TPU v7x, 512 devices: a whole 4x4x16 slice. The times are simulated.
512 devices in a mesh: clip: 32 (over x_hi, z), frame: 16 (over y, x_lo, core).
Axes of the slice: x: 4 (x_hi: 2, x_lo: 2; x = x_hi * 2 + x_lo), y: 4, z: 16, core: 2. Of those that a mesh axis runs over, the one named last changes fastest.
Arguments:
- clips: bfloat16 [32, 16, 16, 32, 256], P('clip', 'frame'), may hold values from -25 to 25, as said below
- cotangent: bfloat16 [32, 16, 16, 32, 256], P('clip', 'frame'), may hold values from -25 to 25
- norm_gain: float32 [256], replicated, may hold values from 0.25 to 1.75
- norm_shift: float32 [256], replicated, may hold values from -3 to 3
- w_spatial: bfloat16 [3, 3, 256, 256], replicated, may hold values from -0.125 to 0.125
- w_time: bfloat16 [3, 256, 256], replicated, may hold values from -0.21875 to 0.21875
Outputs:
- result_video: bfloat16 [32, 16, 16, 32, 256], P('clip', 'frame')
- input_grad: bfloat16 [32, 16, 16, 32, 256], P('clip', 'frame')
- spatial_grad: bfloat16 [3, 3, 256, 256], P(None, None, 'frame')
- time_grad: bfloat16 [3, 256, 256], P(None, 'frame')
Inputs may be any that keep to these rules, and one draw needn't show every extreme that they name: `clips`: input activations.
All inputs are finite; a program needn't handle non-finite values.
Results may differ from a plain program's by a relative error of at most 0.0029.
Values may be sent and summed in bfloat16 or wider, within the bound.
A program may use at most 64 MiB of HBM per device.

v0:
```python
import math
import jax
import jax.numpy as jnp
from jax import lax
from jax.sharding import PartitionSpec as P

GROUPS = 32
epsilon = 1e-05


def group_sums(values, groups):
    return values.reshape(groups, -1).sum(axis=1)


def spread_groups(values, channels):
    return jnp.repeat(values, channels // values.shape[0])


def spatial_conv(hidden, weights):
    row_count, col_count, channels = (hidden.shape[1], hidden.shape[2], hidden.shape[3])
    padded = jnp.pad(hidden, ((0, 0), (1, 1), (1, 1), (0, 0)))
    running = jnp.zeros((hidden.shape[0] * row_count * col_count, weights.shape[-1]), jnp.float32)
    for row_tap in range(3):
        for col_tap in range(3):
            window = padded[
                :, row_tap : row_tap + row_count, col_tap : col_tap + col_count, :
            ].reshape(-1, channels)
            running = running + jnp.dot(
                window, weights[row_tap, col_tap], preferred_element_type=jnp.float32
            )
    return running.reshape(hidden.shape[:-1] + (weights.shape[-1],))


def spatial_weights(hidden, gradient):
    row_count, col_count, channels = (hidden.shape[1], hidden.shape[2], hidden.shape[3])
    padded = jnp.pad(hidden, ((0, 0), (1, 1), (1, 1), (0, 0)))
    flat_grad = gradient.reshape(-1, gradient.shape[-1])
    rows_out = []
    for row_tap in range(3):
        cols_out = []
        for col_tap in range(3):
            window = padded[
                :, row_tap : row_tap + row_count, col_tap : col_tap + col_count, :
            ].reshape(-1, channels)
            cols_out.append(jnp.dot(window.T, flat_grad, preferred_element_type=jnp.float32))
        rows_out.append(jnp.stack(cols_out))
    return jnp.stack(rows_out)


def causal_conv(sequence, w_time):
    frames, channels = (sequence.shape[0], sequence.shape[-1])
    padded = jnp.pad(sequence, ((2, 0),) + ((0, 0),) * (sequence.ndim - 1))
    running = jnp.zeros((sequence.size // channels, channels), jnp.float32)
    for offset in range(3):
        running = running + jnp.dot(
            padded[2 - offset : 2 - offset + frames].reshape(-1, channels),
            w_time[offset],
            preferred_element_type=jnp.float32,
        )
    return running.reshape(sequence.shape)


def causal_back(gradient, w_time):
    frames, channels = (gradient.shape[0], gradient.shape[-1])
    padded = jnp.pad(gradient, ((0, 2),) + ((0, 0),) * (gradient.ndim - 1))
    running = jnp.zeros((gradient.size // channels, channels), jnp.float32)
    for offset in range(3):
        running = running + jnp.dot(
            padded[offset : offset + frames].reshape(-1, channels),
            w_time[offset].T,
            preferred_element_type=jnp.float32,
        )
    return running.reshape(gradient.shape)


def causal_weights(sequence, gradient):
    frames, channels = (sequence.shape[0], sequence.shape[-1])
    padded = jnp.pad(sequence, ((2, 0),) + ((0, 0),) * (sequence.ndim - 1))
    flat_grad = gradient.reshape(-1, channels)
    return jnp.stack(
        [
            jnp.dot(
                padded[2 - offset : 2 - offset + frames].reshape(-1, channels).T,
                flat_grad,
                preferred_element_type=jnp.float32,
            )
            for offset in range(3)
        ]
    )


def per_device(clips, cotangent, norm_gain, norm_shift, w_spatial, w_time):
    frame_count = lax.axis_size("frame")
    clip_count = lax.axis_size("clip")
    video_frame = clips[0]
    grad_frame = cotangent[0]
    row_count, col_count, channels = (
        video_frame.shape[1],
        video_frame.shape[2],
        video_frame.shape[3],
    )
    members = frame_count * row_count * col_count * (channels // GROUPS)
    values = video_frame.astype(jnp.float32)
    value_sum = lax.psum(group_sums(jnp.sum(values, axis=(0, 1, 2)), GROUPS), "frame")
    center = value_sum / members
    centered = values - spread_groups(center, channels)
    square_sum = lax.psum(group_sums(jnp.sum(centered * centered, axis=(0, 1, 2)), GROUPS), "frame")
    variance = square_sum / members
    inv_std = lax.rsqrt(variance + epsilon)
    normed = centered * spread_groups(inv_std, channels)
    activation = normed * norm_gain + norm_shift
    hidden = jax.nn.silu(activation).astype(jnp.bfloat16)
    mixed_frame = spatial_conv(hidden, w_spatial).astype(jnp.bfloat16)
    mixed_band, grad_band = (
        lax.all_to_all(mixed_frame[None], "frame", split_axis=2, concat_axis=1, tiled=True),
        lax.all_to_all(cotangent, "frame", split_axis=2, concat_axis=1, tiled=True),
    )
    band_out = causal_conv(mixed_band[0], w_time).astype(jnp.bfloat16)
    back_band = causal_back(grad_band[0], w_time).astype(jnp.bfloat16)
    time_part = causal_weights(mixed_band[0], grad_band[0])
    temporal, mixed_home = (
        lax.all_to_all(band_out[None], "frame", split_axis=1, concat_axis=2, tiled=True),
        lax.all_to_all(back_band[None], "frame", split_axis=1, concat_axis=2, tiled=True),
    )
    mixed_grad = mixed_home[0]
    result_video = (clips.astype(jnp.float32) + temporal.astype(jnp.float32)).astype(jnp.bfloat16)
    spatial_part = spatial_weights(hidden, mixed_grad)
    flipped = jnp.swapaxes(w_spatial[::-1, ::-1], 2, 3)
    hidden_grad = spatial_conv(mixed_grad, flipped)
    sigmoid_act = jax.nn.sigmoid(activation)
    act_grad = hidden_grad * sigmoid_act * (1.0 + activation * (1.0 - sigmoid_act))
    normed_grad = act_grad * norm_gain
    first_sum, second_sum = lax.psum(
        (
            group_sums(jnp.sum(normed_grad, axis=(0, 1, 2)), GROUPS),
            group_sums(jnp.sum(normed_grad * normed, axis=(0, 1, 2)), GROUPS),
        ),
        "frame",
    )
    input_grad = grad_frame.astype(jnp.float32) + spread_groups(inv_std, channels) * (
        normed_grad
        - spread_groups(first_sum / members, channels)
        - normed * spread_groups(second_sum / members, channels)
    )
    stacked = jnp.concatenate([spatial_part.reshape(9, channels, channels), time_part], axis=0)
    grad_share = lax.psum_scatter(stacked, "frame", scatter_dimension=1, tiled=True)
    grad_share = lax.psum(grad_share, "clip")
    grad_scale = 1.0 / math.sqrt(clip_count * frame_count * row_count * col_count)
    grad_share = grad_share * grad_scale
    spatial_out = grad_share[:9].reshape(3, 3, grad_share.shape[1], channels).astype(jnp.bfloat16)
    time_out = grad_share[9:].astype(jnp.bfloat16)
    return (result_video, input_grad.astype(jnp.bfloat16)[None], spatial_out, time_out)


def solution(mesh):
    placed = (
        P("clip", "frame", None, None, None),
        P("clip", "frame", None, None, None),
        P(),
        P(),
        P(),
        P(),
    )
    return jax.shard_map(
        per_device,
        mesh=mesh,
        in_specs=placed,
        out_specs=(
            P("clip", "frame", None, None, None),
            P("clip", "frame", None, None, None),
            P(None, None, "frame", None),
            P(None, "frame", None),
        ),
        check_vma=False,
    )
```

profile of v0, /device:TPU:8, one launch (start us, length us, event | category | flops | bytes accessed | tf_op | source)
XLA Modules:
  0.0 527.7 jit_solution(11038506905976836317)
XLA Ops:
  7.2 9.3 %all-to-all-start.2 = ((bf16[1,1,16,32,256]{4,3,1,0,2:T(8,128)(2,1)}), bf16[1,1,16,32,256]{4,3,1,0,2:T(8,128)(2,1)S(1)}, u32[]{:S(2)}, u32[]{:S(2)}) async-start(bf16[1,1,16,32,256]{4,3,1,0,2:T(8,128)(2,1)} %bitcast.264), calls=%async_computation.2 | async-start | bytes 524288 | tf_op jit(solution)/shard_map/all_to_all | solution.py:116
  16.5 1.0 convert_reduce_fusion
  17.7 23.8 %psum.35 = f32[32]{0:T(128)S(1)} all-reduce(f32[32]{0:T(128)S(1)} %reduce_sum.73), channel_id=1, replica_groups=mesh['clip'=32,'frame'=16] {'frame'}, use_global_device_ids=true, to_apply=%region_2.0 | all-reduce | flops 32 | bytes 256 | tf_op jit(solution)/shard_map/psum | solution.py:104
  41.7 1.1 multiply_reduce_fusion.1
  43.0 27.1 %psum.36 = f32[32]{0:T(128)S(1)} all-reduce(f32[32]{0:T(128)S(1)} %reduce_sum.75), channel_id=1, replica_groups=mesh['clip'=32,'frame'=16] {'frame'}, use_global_device_ids=true, to_apply=%region_5.0 | all-reduce | flops 32 | bytes 256 | tf_op jit(solution)/shard_map/psum | solution.py:107
  70.6 1.0 pad_slice_fusion.8
  71.9 1.2 reverse_bitcast_fusion
  73.6 1.1 convolution_add_fusion.18
  74.7 1.2 fusion.12
  76.2 1.0 fusion.2
  77.2 10.6 %all-to-all-start.3 = ((bf16[1,16,1,32,256]{4,3,2,0,1:T(8,128)(2,1)}), bf16[1,16,1,32,256]{4,3,2,0,1:T(8,128)(2,1)S(1)}, u32[]{:S(2)}, u32[]{:S(2)}) async-start(bf16[1,16,1,32,256]{4,3,2,0,1:T(8,128)(2,1)} %bitcast.266), calls=%async_computation.3 | async-start | bytes 524288 | tf_op jit(solution)/shard_map/all_to_all | solution.py:123
  87.8 2.2 convolution_add_fusion.17
  90.0 3.3 all-to-all-done.3
  93.3 1.9 convolution_bitcast_fusion.8
  95.2 1.9 convolution_bitcast_fusion.9
  97.2 1.9 convolution_bitcast_fusion.10
  99.1 1.0 convolution_bitcast_fusion.11
  100.3 1.0 copy-done.2
  103.4 1.2 fusion.41
  105.1 24.8 %all-reduce.4 = (f32[32]{0:T(128)S(1)}, f32[32]{0:T(128)S(1)}) all-reduce(f32[32]{0:T(128)S(1)} %reduce_sum.79, f32[32]{0:T(128)S(1)} %reduce_sum.77), channel_id=1, replica_groups=mesh['clip'=32,'frame'=16] {'frame'}, use_global_device_ids=true, to_apply=%region_11.12 | all-reduce | flops 64 | bytes 512 | tf_op jit(solution)/shard_map/psum | solution.py:133
  130.2 2.3 add_convert_fusion
  132.5 1.0 convolution_bitcast_fusion.7
  134.7 1.0 convolution_bitcast_fusion.4
  135.9 1.0 convolution_bitcast_fusion.3
  137.8 9.2 %all-to-all-start = ((bf16[1,1,16,32,256]{4,3,1,0,2:T(8,128)(2,1)}), bf16[1,1,16,32,256]{4,3,1,0,2:T(8,128)(2,1)S(1)}, u32[]{:S(2)}, u32[]{:S(2)}) async-start(bf16[1,1,16,32,256]{4,3,1,0,2:T(8,128)(2,1)} %bitcast.265), calls=%async_computation | async-start | bytes 524288 | tf_op jit(solution)/shard_map/all_to_all | solution.py:115
  147.0 1.0 maximum_bitcast_fusion.2
  149.4 3.1 all-to-all-done
  153.4 2.0 pad_maximum_fusion
  155.4 1.0 copy-done.9
  157.8 6.0 %all-to-all-start.1 = ((bf16[1,16,1,32,256]{4,3,2,0,1:T(8,128)(2,1)}), bf16[1,16,1,32,256]{4,3,2,0,1:T(8,128)(2,1)S(1)}, u32[]{:S(2)}, u32[]{:S(2)}) async-start(bf16[1,16,1,32,256]{4,3,2,0,1:T(8,128)(2,1)} %bitcast.29), calls=%async_computation.1 | async-start | bytes 524288 | tf_op jit(solution)/shard_map/all_to_all | solution.py:122
  163.9 59.5 %reduce-scatter.2.cloned.1.call-done = f32[12,16,256]{2,1,0:T(8,128)} async-done(((f32[12,256,256]{2,1,0:T(8,128)}), f32[12,16,256]{2,1,0:T(8,128)}) %reduce-scatter.2.cloned.1.call-update) | async-done | bytes 196624 | tf_op jit(solution)/shard_map/reduce_scatter | solution.py:146
  224.3 294.4 %all-reduce.7.cloned.1.call-done = f32[12,16,256]{2,1,0:T(8,128)} async-done(((f32[12,16,256]{2,1,0:T(8,128)}), f32[12,16,256]{2,1,0:T(8,128)}) %all-reduce.7.cloned.1.call-update) | async-done | bytes 196624 | tf_op jit(solution)/shard_map/psum | solution.py:147
  (94 shorter events, 14.2 us)
Async XLA Ops:
  7.2 63.2 %copy-start = (bf16[1,1,16,32,256]{4,3,2,1,0:T(8,128)(2,1)S(1)}, bf16[1,1,16,32,256]{4,3,2,1,0:T(8,128)(2,1)}, u32[]{:S(2)}) copy-start(bf16[1,1,16,32,256]{4,3,2,1,0:T(8,128)(2,1)} %param.6) | copy-start | bytes 786436
  7.2 63.1 %copy-start.16 = (f32[256]{0:T(256)S(1)}, f32[256]{0:T(256)}, u32[]{:S(2)}) copy-start(f32[256]{0:T(256)} %param.9) | copy-start | bytes 3076
  7.2 63.1 %copy-start.17 = (f32[256]{0:T(256)S(1)}, f32[256]{0:T(256)}, u32[]{:S(2)}) copy-start(f32[256]{0:T(256)} %param.8) | copy-start | bytes 3076
  7.2 67.5 %all-to-all-start.2 = ((bf16[1,1,16,32,256]{4,3,1,0,2:T(8,128)(2,1)}), bf16[1,1,16,32,256]{4,3,1,0,2:T(8,128)(2,1)S(1)}, u32[]{:S(2)}, u32[]{:S(2)}) async-start(bf16[1,1,16,32,256]{4,3,1,0,2:T(8,128)(2,1)} %bitcast.264), calls=%async_computation.2 | async-start | bytes 524288 | tf_op jit(solution)/shard_map/all_to_all | solution.py:116
  70.5 1.4 copy-start.1
  71.9 1.7 copy-start.3
  71.9 1.7 copy-start.4
  74.7 1.3 copy-start.8
  77.2 16.1 %all-to-all-start.3 = ((bf16[1,16,1,32,256]{4,3,2,0,1:T(8,128)(2,1)}), bf16[1,16,1,32,256]{4,3,2,0,1:T(8,128)(2,1)S(1)}, u32[]{:S(2)}, u32[]{:S(2)}) async-start(bf16[1,16,1,32,256]{4,3,2,0,1:T(8,128)(2,1)} %bitcast.266), calls=%async_computation.3 | async-start | bytes 524288 | tf_op jit(solution)/shard_map/all_to_all | solution.py:123
  100.0 1.3 copy-start.2
  130.2 3.2 copy-start.7
  135.9 11.1 %copy-start.15 = (f32[1,256,256]{2,1,0:T(8,128)S(1)}, f32[1,256,256]{2,1,0:T(8,128)}, u32[]{:S(2)}) copy-start(f32[1,256,256]{2,1,0:T(8,128)} %convolution_bitcast_fusion.4) | copy-start | bytes 786436
  137.8 10.2 %copy-start.12 = (f32[1,256,256]{2,1,0:T(8,128)S(1)}, f32[1,256,256]{2,1,0:T(8,128)}, u32[]{:S(2)}) copy-start(f32[1,256,256]{2,1,0:T(8,128)} %convolution_bitcast_fusion.8) | copy-start | bytes 786436
  137.8 10.3 %copy-start.14 = (f32[1,256,256]{2,1,0:T(8,128)S(1)}, f32[1,256,256]{2,1,0:T(8,128)}, u32[]{:S(2)}) copy-start(f32[1,256,256]{2,1,0:T(8,128)} %convolution_bitcast_fusion.7) | copy-start | bytes 786436
  137.8 14.7 %all-to-all-start = ((bf16[1,1,16,32,256]{4,3,1,0,2:T(8,128)(2,1)}), bf16[1,1,16,32,256]{4,3,1,0,2:T(8,128)(2,1)S(1)}, u32[]{:S(2)}, u32[]{:S(2)}) async-start(bf16[1,1,16,32,256]{4,3,1,0,2:T(8,128)(2,1)} %bitcast.265), calls=%async_computation | async-start | bytes 524288 | tf_op jit(solution)/shard_map/all_to_all | solution.py:115
  147.0 76.5 %reduce-scatter.2.cloned.1.call-start = ((), (), s32[]{:S(2)}) async-start(), calls=%async_computation.5 | async-start | bytes 3342336 | tf_op jit(solution)/shard_map/reduce_scatter | solution.py:146
  148.0 1.0 copy-start.10
  148.1 1.0 copy-start.11
  148.1 1.1 copy-start.13
  152.5 0.8 copy-start.5
  155.4 1.0 copy-start.9
  155.4 1.2 copy-start.6
  157.8 65.7 %all-to-all-start.1 = ((bf16[1,16,1,32,256]{4,3,2,0,1:T(8,128)(2,1)}), bf16[1,16,1,32,256]{4,3,2,0,1:T(8,128)(2,1)S(1)}, u32[]{:S(2)}, u32[]{:S(2)}) async-start(bf16[1,16,1,32,256]{4,3,2,0,1:T(8,128)(2,1)} %bitcast.29), calls=%async_computation.1 | async-start | bytes 524288 | tf_op jit(solution)/shard_map/all_to_all | solution.py:122
  163.8 354.8 %all-reduce.7.cloned.1.call-start = ((), (), s32[]{:S(2)}) async-start(), calls=%async_computation.6 | async-start | bytes 393216 | tf_op jit(solution)/shard_map/psum | solution.py:147
Sparse Core Ops, SparseCore 0:
  155.6 67.8 reduce-scatter.1
  226.3 292.2 all-reduce.6
where the time goes:
time: 529 us; the launch traced here: 528 us
  waiting for transfers between devices  360 us (68%)
  blocking collectives  75.7 us (14%)
  starting transfers between devices  35.2 us (7%)
  matrix products  23.5 us (4%)
  between operations  14.5 us (3%)
  other arithmetic  10.1 us (2%)
  local copies, waits for them, and re-layouts  8.18 us (2%)
    psum x1, waiting for transfers between devices, per_device(): grad_share = lax.psum(grad_share, 'clip')  294 us
    reduce_scatter x1, waiting for transfers between devices, per_device(): lax.psum_scatter(stacked, 'frame', scatter_dimension=1, tiled=True)  59.5 us
    psum x1, blocking collectives, per_device(): lax.psum(group_sums(jnp.sum(centered * centered, axis=(0, 1, 2)), GROUPS)...  27.1 us
    psum x1, blocking collectives, per_device(): lax.psum((group_sums(jnp.sum(normed_grad, axis=(0, 1, 2)), GROUPS), group...  24.8 us
    psum x1, blocking collectives, per_device(): lax.psum(group_sums(jnp.sum(values, axis=(0, 1, 2)), GROUPS), 'frame')  23.8 us
    all_to_all x1, starting transfers between devices, per_device(): lax.all_to_all(back_band[None], 'frame', split_axis=1, concat_axis=2, til...  10.6 us
  transfers between devices with their start and end apart: 6, of which 4 were waited for; matrix products, arithmetic and copies ran while one was open for 2% of the time, Pallas kernels for 0%

commit v1 on v0

--- a/solution.py
+++ b/solution.py
@@ -3,9 +3,15 @@
 import jax.numpy as jnp
 from jax import lax
 from jax.sharding import PartitionSpec as P
+from jax.lax import all_gather
 
 GROUPS = 32
 epsilon = 1e-05
+
+
+def form_the_blocks(chunk, comm_axis):
+    back = all_gather(chunk, comm_axis).sum(axis=0)
+    return back
 
 
 def group_sums(values, groups):
@@ -144,7 +150,7 @@
     )
     stacked = jnp.concatenate([spatial_part.reshape(9, channels, channels), time_part], axis=0)
     grad_share = lax.psum_scatter(stacked, "frame", scatter_dimension=1, tiled=True)
-    grad_share = lax.psum(grad_share, "clip")
+    grad_share = form_the_blocks(grad_share, "clip")
     grad_scale = 1.0 / math.sqrt(clip_count * frame_count * row_count * col_count)
     grad_share = grad_share * grad_scale
     spatial_out = grad_share[:9].reshape(3, 3, grad_share.shape[1], channels).astype(jnp.bfloat16)

time: 529 us -> 421 us (0.80)
  the two profiles are of different devices: /device:TPU:8 before, /device:TPU:32 now
where the time goes in v1:
time: 421 us; the launch traced here: 420 us
  waiting for transfers between devices  257 us (61%)
  blocking collectives  96.5 us (23%)
  matrix products  20.6 us (5%)
  between operations  14.6 us (3%)
  starting transfers between devices  12.9 us (3%)
  other arithmetic  12.5 us (3%)
  local copies, waits for them, and re-layouts  6.79 us (2%)
    all_gather x1, waiting for transfers between devices, form_the_blocks(): back = all_gather(chunk, comm_axis).sum(axis=0)  169 us
    reduce_scatter x1, waiting for transfers between devices, per_device(): lax.psum_scatter(stacked, 'frame', scatter_dimension=1, tiled=True)  76.1 us
    psum x1, blocking collectives, per_device(): lax.psum(group_sums(jnp.sum(values, axis=(0, 1, 2)), GROUPS), 'frame')  30.9 us
    psum x1, blocking collectives, per_device(): lax.psum((group_sums(jnp.sum(normed_grad, axis=(0, 1, 2)), GROUPS), group...  27.8 us
    psum x1, blocking collectives, per_device(): lax.psum(group_sums(jnp.sum(centered * centered, axis=(0, 1, 2)), GROUPS)...  27.1 us
    all_to_all x1, blocking collectives, per_device(): lax.all_to_all(band_out[None], 'frame', split_axis=1, concat_axis=2, tile...  10.6 us
    dot_general x18, matrix products, spatial_conv(): jnp.dot(window, weights[row_tap, col_tap], preferred_element_type=jnp.flo...  8.82 us
  transfers between devices with their start and end apart: 5, of which 4 were waited for; matrix products, arithmetic and copies ran while one was open for 3% of the time, Pallas kernels for 0%

profile of v1, /device:TPU:32, one launch (start us, length us, event | category | flops | bytes accessed | tf_op | source)
XLA Modules:
  0.0 420.4 jit_solution(5305713201452121018)
XLA Ops:
  7.2 5.6 %all-to-all-start.2 = ((bf16[1,1,16,32,256]{4,3,1,0,2:T(8,128)(2,1)}), bf16[1,1,16,32,256]{4,3,1,0,2:T(8,128)(2,1)S(1)}, u32[]{:S(2)}, u32[]{:S(2)}) async-start(bf16[1,1,16,32,256]{4,3,1,0,2:T(8,128)(2,1)} %bitcast.266), calls=%async_computation.2 | async-start | bytes 524288 | tf_op jit(solution)/shard_map/all_to_all | solution.py:122
  12.9 1.0 convert_reduce_fusion
  14.1 30.9 %psum.28 = f32[32]{0:T(128)S(1)} all-reduce(f32[32]{0:T(128)S(1)} %reduce_sum.82), channel_id=1, replica_groups=mesh['clip'=32,'frame'=16] {'frame'}, use_global_device_ids=true, to_apply=%region_2.0 | all-reduce | flops 32 | bytes 256 | tf_op jit(solution)/shard_map/psum | solution.py:110
  45.2 1.1 multiply_reduce_fusion.1
  46.5 27.1 %psum.29 = f32[32]{0:T(128)S(1)} all-reduce(f32[32]{0:T(128)S(1)} %reduce_sum.84), channel_id=1, replica_groups=mesh['clip'=32,'frame'=16] {'frame'}, use_global_device_ids=true, to_apply=%region_5.0 | all-reduce | flops 32 | bytes 256 | tf_op jit(solution)/shard_map/psum | solution.py:113
  74.0 1.2 pad_slice_fusion.8
  76.7 1.0 convolution_add_fusion.18
  77.8 1.2 fusion.12
  79.3 1.0 fusion.2
  80.2 3.5 all-to-all-start.3
  83.8 2.2 convolution_add_fusion.17
  85.9 5.9 %all-to-all-done.3 = bf16[1,16,1,32,256]{4,3,2,0,1:T(8,128)(2,1)S(1)} async-done(((bf16[1,16,1,32,256]{4,3,2,0,1:T(8,128)(2,1)}), bf16[1,16,1,32,256]{4,3,2,0,1:T(8,128)(2,1)S(1)}, u32[]{:S(2)}, u32[]{:S(2)}) %all-to-all-start.3) | async-done | bytes 262176 | tf_op jit(solution)/shard_map/all_to_all | solution.py:129
  91.8 2.0 convolution_bitcast_fusion.8
  93.7 1.9 convolution_bitcast_fusion.9
  95.7 1.0 convolution_bitcast_fusion.10
  96.7 1.0 convolution_bitcast_fusion.11
  100.1 1.3 fusion.41
  101.8 27.8 %all-reduce.4 = (f32[32]{0:T(128)S(1)}, f32[32]{0:T(128)S(1)}) all-reduce(f32[32]{0:T(128)S(1)} %reduce_sum.88, f32[32]{0:T(128)S(1)} %reduce_sum.86), channel_id=1, replica_groups=mesh['clip'=32,'frame'=16] {'frame'}, use_global_device_ids=true, to_apply=%region_11.12 | all-reduce | flops 64 | bytes 512 | tf_op jit(solution)/shard_map/psum | solution.py:139
  129.9 2.2 add_convert_fusion
  135.1 1.0 convolution_bitcast_fusion.3
  136.1 0.9 fusion
  137.0 3.7 all-to-all-start
  140.7 1.0 maximum_bitcast_fusion.2
  141.8 0.9 copy-done.14
  143.1 5.6 %all-to-all-done = bf16[1,1,16,32,256]{4,3,1,0,2:T(8,128)(2,1)S(1)} async-done(((bf16[1,1,16,32,256]{4,3,1,0,2:T(8,128)(2,1)}), bf16[1,1,16,32,256]{4,3,1,0,2:T(8,128)(2,1)S(1)}, u32[]{:S(2)}, u32[]{:S(2)}) %all-to-all-start) | async-done | bytes 262176 | tf_op jit(solution)/shard_map/all_to_all | solution.py:121
  149.6 2.0 pad_maximum_fusion
  151.7 76.1 %reduce-scatter.2.cloned.1.call-done = f32[12,16,256]{2,1,0:T(8,128)} async-done(((f32[12,256,256]{2,1,0:T(8,128)}), f32[12,16,256]{2,1,0:T(8,128)}) %reduce-scatter.2.cloned.1.call-update) | async-done | bytes 196624 | tf_op jit(solution)/shard_map/reduce_scatter | solution.py:152
  228.5 10.6 %all_to_all.16 = bf16[1,16,1,32,256]{4,3,2,0,1:T(8,128)(2,1)S(1)} all-to-all(bf16[1,16,1,32,256]{4,3,2,0,1:T(8,128)(2,1)S(1)} %bitcast.269), channel_id=1, replica_groups=mesh['clip'=32,'frame'=16] {'frame'}, dimensions={1} | all-to-all | bytes 524288 | tf_op jit(solution)/shard_map/all_to_all | solution.py:128
  239.2 0.8 fusion.3
  239.9 169.0 %all-gather.3.cloned.1.call-done = f32[384,16,256]{2,1,0:T(8,128)} async-done(((f32[12,16,256]{2,1,0:T(8,128)}), f32[384,16,256]{2,1,0:T(8,128)}) %all-gather.3.cloned.1.call-update) | async-done | bytes 6291472 | tf_op jit(solution)/shard_map/all_gather | solution.py:13
  408.9 3.4 reduce_sum.89
  412.4 0.6 slice.202
  (100 shorter events, 11.4 us)
Async XLA Ops:
  7.2 66.6 %copy-start = (bf16[1,1,16,32,256]{4,3,2,1,0:T(8,128)(2,1)S(1)}, bf16[1,1,16,32,256]{4,3,2,1,0:T(8,128)(2,1)}, u32[]{:S(2)}) copy-start(bf16[1,1,16,32,256]{4,3,2,1,0:T(8,128)(2,1)} %param.6) | copy-start | bytes 786436
  7.2 66.6 %copy-start.19 = (f32[256]{0:T(256)S(1)}, f32[256]{0:T(256)}, u32[]{:S(2)}) copy-start(f32[256]{0:T(256)} %param.9) | copy-start | bytes 3076
  7.2 66.6 %copy-start.20 = (f32[256]{0:T(256)S(1)}, f32[256]{0:T(256)}, u32[]{:S(2)}) copy-start(f32[256]{0:T(256)} %param.8) | copy-start | bytes 3076
  7.2 70.5 %all-to-all-start.2 = ((bf16[1,1,16,32,256]{4,3,1,0,2:T(8,128)(2,1)}), bf16[1,1,16,32,256]{4,3,1,0,2:T(8,128)(2,1)S(1)}, u32[]{:S(2)}, u32[]{:S(2)}) async-start(bf16[1,1,16,32,256]{4,3,1,0,2:T(8,128)(2,1)} %bitcast.266), calls=%async_computation.2 | async-start | bytes 524288 | tf_op jit(solution)/shard_map/all_to_all | solution.py:122
  74.0 1.7 copy-start.1
  75.8 0.7 copy-start.6
  75.8 0.9 copy-start.8
  77.7 1.3 copy-start.12
  80.2 11.6 %all-to-all-start.3 = ((bf16[1,16,1,32,256]{4,3,2,0,1:T(8,128)(2,1)}), bf16[1,16,1,32,256]{4,3,2,0,1:T(8,128)(2,1)S(1)}, u32[]{:S(2)}, u32[]{:S(2)}) async-start(bf16[1,16,1,32,256]{4,3,2,0,1:T(8,128)(2,1)} %bitcast.268), calls=%async_computation.3 | async-start | bytes 524288 | tf_op jit(solution)/shard_map/all_to_all | solution.py:129
  91.8 3.9 copy-start.7
  100.1 29.8 %copy-start.18 = (bf16[1,1,16,32,256]{4,3,2,1,0:T(8,128)(2,1)S(1)}, bf16[1,1,16,32,256]{4,3,2,1,0:T(8,128)(2,1)}, u32[]{:S(2)}) copy-start(bf16[1,1,16,32,256]{4,3,2,1,0:T(8,128)(2,1)} %param.7) | copy-start | bytes 786436
  129.9 2.5 copy-start.11
  132.1 0.9 copy-start.5
  132.6 1.0 copy-start.4
  133.6 1.0 copy-start.3
  134.1 1.0 copy-start.2
  137.0 4.7 %copy-start.16 = (f32[1,256,256]{2,1,0:T(8,128)S(1)}, f32[1,256,256]{2,1,0:T(8,128)}, u32[]{:S(2)}) copy-start(f32[1,256,256]{2,1,0:T(8,128)} %convolution_bitcast_fusion.8) | copy-start | bytes 786436
  137.0 11.7 %all-to-all-start = ((bf16[1,1,16,32,256]{4,3,1,0,2:T(8,128)(2,1)}), bf16[1,1,16,32,256]{4,3,1,0,2:T(8,128)(2,1)S(1)}, u32[]{:S(2)}, u32[]{:S(2)}) async-start(bf16[1,1,16,32,256]{4,3,1,0,2:T(8,128)(2,1)} %bitcast.267), calls=%async_computation | async-start | bytes 524288 | tf_op jit(solution)/shard_map/all_to_all | solution.py:121
  140.7 87.1 %reduce-scatter.2.cloned.1.call-start = ((), (), s32[]{:S(2)}) async-start(), calls=%async_computation.5 | async-start | bytes 3342336 | tf_op jit(solution)/shard_map/reduce_scatter | solution.py:152
  141.7 1.0 copy-start.14
  141.8 1.0 copy-start.15
  141.8 1.1 copy-start.17
  148.7 0.8 copy-start.9
  151.6 76.2 %copy-start.13 = (bf16[3,256,256]{2,1,0:T(8,128)(2,1)S(1)}, bf16[3,256,256]{2,1,0:T(8,128)(2,1)}, u32[]{:S(2)}) copy-start(bf16[3,256,256]{2,1,0:T(8,128)(2,1)} %param.11) | copy-start | bytes 1179652
  151.6 76.4 %copy-start.10 = (bf16[16,1,32,256]{3,2,0,1:T(8,128)(2,1)S(1)}, bf16[16,1,32,256]{3,2,0,1:T(8,128)(2,1)}, u32[]{:S(2)}) copy-start(bf16[16,1,32,256]{3,2,0,1:T(8,128)(2,1)} %copy-done.9) | copy-start | bytes 786436
  151.7 257.3 %all-gather.3.cloned.1.call-start = ((), (), s32[]{:S(2)}) async-start(), calls=%async_computation.6 | async-start | bytes 6488064 | tf_op jit(solution)/shard_map/all_gather | solution.py:13
Sparse Core Ops, SparseCore 0:
  151.8 75.9 reduce-scatter.1
  230.9 178.0 all-gather.2
